TPU v7x, 128 devices: a whole 4x4x4 slice. The times are simulated.
128 devices in a mesh: tm: 8 (over z, core), space: 16 (over y, x).
Axes of the slice: x: 4, y: 4, z: 4, core: 2. Of those that a mesh axis runs over, the one named last changes fastest.
Arguments:
- init_field: float32 [2, 128, 1024], P(None, 'space'), may hold values from -3 to 3
- guess: float32 [256, 2, 128, 1024], P('tm', None, 'space'), may hold values from -3 to 3
- slab_blocks: int32 [8], replicated, may hold values from 1 to 4, 16 in all
Outputs:
- updated: float32 [256, 2, 128, 1024], P('tm', None, 'space')
Inputs may be any that keep to these rules, and one draw needn't show every extreme that they name: slab_blocks sums to 16; some slab holds exactly 4.
All inputs are finite; a program needn't handle non-finite values.
Results may differ from a plain program's by a relative error of at most 0.000028.
Values sent between devices are 32-bit elements; how exact they have to be, the bound alone decides.
No kernel may reach another device: no remote copies, remote signals or barrier semaphores. Data moves between devices by JAX's collectives and lax.ppermute only.
A program may use at most 128 MiB of HBM per device.

v0:
```python
import jax
import jax.numpy as jnp
from jax import lax
from jax.experimental import pallas as pl
from jax.experimental.pallas import tpu as pltpu
from jax.sharding import PartitionSpec as P

diffusion_rate = (0.0035, 0.028, 0.224)
advection_rate = (0.003, 0.024, 0.192)
F32 = jnp.float32

SNAKE = [4 * (s // 4) + (s % 4 if (s // 4) % 2 == 0 else 3 - s % 4) for s in range(16)]
SMEM = pl.BlockSpec(memory_space=pltpu.SMEM)
VMEM = pl.BlockSpec(memory_space=pltpu.VMEM)
SINGLE = (2, 16, 8, 128)
QUAD = (2, 4, 16, 8, 128)


def shape(*dims):
    return jax.ShapeDtypeStruct(dims, F32)


def whole(kernel, outs, inputs, microseconds, scratch=(), grid=()):
    specs = [VMEM] * inputs if isinstance(inputs, int) else [VMEM if x is None else x for x in inputs]
    return pl.pallas_call(
        kernel,
        grid=grid,
        out_shape=outs,
        in_specs=[SMEM] + specs,
        out_specs=jax.tree.map(lambda _: VMEM, outs),
        scratch_shapes=list(scratch),
        compiler_params=pltpu.CompilerParams(vmem_limit_bytes=12 * 1024 * 1024),
        cost_estimate=pl.CostEstimate(
            flops=microseconds * 10**9, bytes_accessed=microseconds * 3 * 10**6, transcendentals=0
        ),
        name=kernel.__name__,
    )


def lanes():
    return lax.broadcasted_iota(jnp.int32, (8, 128), 1)


def picked(u, index):
    return jnp.take_along_axis(u, index, axis=1, mode="promise_in_bounds")


def exchanged(tiles, sizes, first=0):
    tiles, lane = list(tiles), (lanes() + 128 - first) % 128
    apart = len(tiles) // 2
    for size in sizes:
        lower = (lane // size) % 2 == 0
        for a in range(len(tiles)):
            if (a // apart) % 2 == 0:
                x, y = tiles[a], tiles[a + apart]
                tiles[a] = jnp.where(lower, x, pltpu.roll(y, size, 1))
                tiles[a + apart] = jnp.where(lower, pltpu.roll(x, 128 - size, 1), y)
        apart //= 2
    return tiles


def quad_order():
    lane = lanes()
    return 4 * (lane % 32) + lane // 32


def single_order():
    lane = lanes()
    return 32 * (lane % 4) + lane // 4


def step(p, q, level):
    d = diffusion_rate[level]
    sub = lax.broadcasted_iota(jnp.int32, (8, 128), 0)
    wp, ep, sq, nq = d + p, d - p, d + q, d - q

    def one(u):
        after_last = jnp.where(sub == 7, 0.0, pltpu.roll(u[0], 7, 0))
        before_first = jnp.where(sub == 0, 0.0, pltpu.roll(u[15], 1, 0))
        north = jnp.concatenate([u[1:], after_last[None]], 0)
        south = jnp.concatenate([before_first[None], u[:-1]], 0)
        east = pltpu.roll(u, 127, 2)
        west = pltpu.roll(u, 1, 2)
        return (1.0 - 4.0 * d) * u + ep * east + wp * west + nq * north + sq * south

    return one(p), one(q)


def quad_step(read, write, level):
    d = diffusion_rate[level]
    sub = lax.broadcasted_iota(jnp.int32, (8, 128), 0)

    def row(k):
        return [[read(c, j, k) for j in range(4)] for c in range(2)]

    first = row(0)
    south = [[jnp.where(sub == 0, 0.0, pltpu.roll(u, 1, 0)) for u in us] for us in row(15)]
    beyond = [[jnp.where(sub == 7, 0.0, pltpu.roll(u, 7, 0)) for u in us] for us in first]
    here = first
    for k in range(16):
        north = row(k + 1) if k < 15 else beyond
        edge_east = [pltpu.roll(us[0], 127, 1) for us in here]
        edge_west = [pltpu.roll(us[3], 1, 1) for us in here]
        for j in range(4):
            p, q = here[0][j], here[1][j]
            wp, ep, sq, nq = d + p, d - p, d + q, d - q
            made = []
            for c in range(2):
                east = here[c][j + 1] if j < 3 else edge_east[c]
                west = here[c][j - 1] if j > 0 else edge_west[c]
                made.append(
                    ((1.0 - 4.0 * d) * here[c][j] + ep * east)
                    + (wp * west + nq * north[c][j])
                    + sq * south[c][j]
                )
            write(j, k, *made)
        south, here = here, north


def reader(ref, *lead):
    return lambda c, j, k: ref[(*lead, c, j, k)]


def writer(ref, *lead):
    def write(j, k, p, q):
        ref[(*lead, 0, j, k)] = p
        ref[(*lead, 1, j, k)] = q

    return write


def adder(ref, g, t):
    def write(j, k, p, q):
        ref[0, j, k] = p + g[t, 0, j, k]
        ref[1, j, k] = q + g[t, 1, j, k]

    return write


def eight_forced_steps(a, b, g):
    @pl.loop(0, 4)
    def _(n):
        quad_step(reader(a), adder(b, g, 2 * n), 1)
        quad_step(reader(b), adder(a, g, 2 * n + 1), 1)


def rows_loop(body):
    pl.loop(0, 16, unroll=8)(body)


def in_each(body):
    @rows_loop
    def _(k):
        for c in range(2):
            for j in range(4):
                body(c, j, k)


def windows_kernel(nb):
    number = 2 * nb

    def kernel(slab_blocks, guess, init, out, made):
        slab = lax.axis_index("tm")
        blocks = slab_blocks[slab]
        lane = lanes()
        beyond = (lane >= 96, lane < 32)

        def tile(i, at, m):
            n, c = m // 2, m % 2
            last_c_point = (slab == 7) & (n == number - 1)
            cols = slice(128 * at, 128 * at + 128)
            if nb == 3:
                block, w = (i, n) if i < 3 else (n % 3, 6 + n // 3)
                special = last_c_point if i == 3 else None
            else:
                block, w = i % nb, n + number * (i // nb)
                special = last_c_point & (block == blocks - 1) if i // nb == 4 // nb - 1 else None
            u = guess[8 * block + w, c, :, cols]
            return u if special is None else jnp.where(special, init[c, :, cols], u)

        for odd in range(2):
            order = (quad_order() + 96 + 64 * odd) % 128

            @pl.loop(0, 2 * number, unroll=4)
            def _(m):
                for i in range(4):
                    for at in range(8):
                        u = jnp.where(beyond[odd], tile(i, (at + 7 + 2 * odd) % 8, m), tile(i, at, m))
                        made[odd, m, i, at] = picked(advection_rate[0] * u, order)

        for size in (64, 32):
            apart = size // 32
            lower = lane // size % 2 == 0

            @pl.loop(0, 2 * number, unroll=4)
            def _(m):
                for odd in range(2):
                    for at in range(8):
                        for x in range(4):
                            if x // apart % 2 == 0:
                                p, q = made[odd, m, x, at], made[odd, m, x + apart, at]
                                p, q = (
                                    jnp.where(lower, p, pltpu.roll(q, size, 1)),
                                    jnp.where(lower, pltpu.roll(p, 128 - size, 1), q),
                                )
                                if size == 64:
                                    made[odd, m, x, at] = p
                                    made[odd, m, x + apart, at] = q
                                else:
                                    out[SNAKE[2 * at + odd], m // 2, m % 2, x] = p
                                    out[SNAKE[2 * at + odd], m // 2, m % 2, x + apart] = q

    kernel.__name__ = "windows_kernel"
    return kernel


def gather_kernel(nb):
    def kernel(slab_blocks, packed, out):
        group = lanes() // 32

        @pl.loop(0, 16 * packed.shape[2], unroll=8)
        def _(m):
            source, x = m // packed.shape[2], m % packed.shape[2]
            us = [packed[source, n, x] for n in range(2 * nb)]
            for n in range(2 * nb):
                out[source, n, x] = us[n]
            for w in range(2):
                if nb == 3:
                    first, second, third = us[3 * w : 3 * w + 3]
                    u = jnp.where(group == 1, pltpu.roll(second, 64, 1), pltpu.roll(first, 32, 1))
                    u = jnp.where(group == 2, pltpu.roll(third, 96, 1), u)
                else:
                    u = pltpu.roll(us[2 * nb - 2 + w], 32 * nb, 1)
                out[source, 6 + w, x] = u

    kernel.__name__ = "gather_kernel"
    return kernel


def spread_kernel(nb):
    number = 2 * nb

    def kernel(slab_blocks, packed, out):
        group = (lanes() + 120) % 128 // 32
        if nb == 3:

            @pl.loop(0, 16 * packed.shape[2], unroll=8)
            def _(m):
                source, x = m // packed.shape[2], m % packed.shape[2]
                us = [packed[source, n, x] for n in range(6)]
                for n in range(6):
                    out[source, n, x] = us[n]
                for w in range(2):
                    first, second, third = us[3 * w : 3 * w + 3]
                    u = jnp.where(group == 1, pltpu.roll(second, 64, 1), pltpu.roll(first, 32, 1))
                    out[source, 6 + w, x] = jnp.where(group == 2, pltpu.roll(third, 96, 1), u)

            return

        @pl.loop(0, 16 * number, unroll=8)
        def _(m):
            source, n = m // number, m % number
            for x in range(packed.shape[2]):
                u = packed[source, n, x]
                for r in range(4 // nb):
                    out[source, n + number * r, x] = pltpu.roll(u, 128 - 32 * nb * r, 1) if r else u

    kernel.__name__ = "spread_kernel"
    return kernel


def pack_kernel(nb):
    number = 2 * nb

    def kernel(slab_blocks, full, out):
        group = (lanes() + 120) % 128 // (32 if nb == 3 else 32 * nb)
        if nb == 3:

            @pl.loop(0, 16 * full.shape[2], unroll=8)
            def _(m):
                target, x = m // full.shape[2], m % full.shape[2]
                for n in range(6):
                    u = pltpu.roll(full[target, 6 + n // 3, x], 96 - 32 * (n % 3), 1)
                    out[target, n, x] = jnp.where(group == 3, u, full[target, n, x])

            return

        @pl.loop(0, 16 * number, unroll=8)
        def _(m):
            target, n = m // number, m % number
            for x in range(full.shape[2]):
                u = full[target, n, x]
                for r in range(1, 4 // nb):
                    u = jnp.where(group == r, pltpu.roll(full[target, n + number * r, x], 32 * nb * r, 1), u)
                out[target, n, x] = u

    kernel.__name__ = "pack_kernel"
    return kernel


def taker(points):
    number = points.shape[1]
    flat = points.reshape(16 * number * 64, 128)

    def taken(n, c, j, k):
        first = (k // 8) * number * 64 + n * 64 + c * 32 + j * 8 + k % 8
        return flat[pl.ds(first, 8, stride=number * 128), :]

    return taken


def tail_kernel(slab_blocks, points, out):
    lane = lanes()
    taken = taker(points)
    shift = 128 - 32 * (slab_blocks[lax.axis_index("tm")] - 1)

    @rows_loop
    def _(k):
        for n in range(2):
            for c in range(2):
                u = pltpu.roll(taken(n, c, 0, k), shift % 128, 1)
                for j in range(1, 4):
                    u = jnp.where(lane // 32 == j, pltpu.roll(taken(n, c, j, k), (shift + 32 * j) % 128, 1), u)
                out[n, c, k] = u


def chain(load, a, b, g, t, middle):
    def six_steps(x, y):
        @pl.loop(0, 3)
        def _(_):
            quad_step(reader(x), writer(y), 0)
            quad_step(reader(y), writer(x), 0)

    def finish(j, k, p, q):
        g[t, 0, j, k] = 8.0 * p - g[t, 0, j, k]
        g[t, 1, j, k] = 8.0 * q - g[t, 1, j, k]

    quad_step(load, writer(b), 0)
    six_steps(b, a)
    quad_step(reader(b), writer(a), 0)
    middle()
    quad_step(lambda c, j, k: 8.0 * a[c, j, k], writer(g, t), 1)
    six_steps(a, b)
    quad_step(reader(a), writer(b), 0)
    quad_step(reader(b), finish, 0)


def inner_fine_kernel(slab_blocks, points, g, a, b):
    taken = taker(points)
    blocks = slab_blocks[lax.axis_index("tm")]

    @pl.loop(0, jnp.minimum(2 * blocks, 6))
    def _(t):
        chain(lambda c, j, k: taken(t, c, j, k), a, b, g, t, lambda: None)

    def spread(target, source, shift):
        @in_each
        def _(c, j, k):
            g[target, c, j, k] = pltpu.roll(g[source, c, j, k], shift, 1)

    @pl.when(blocks == 2)
    def _():
        @pl.loop(0, 2)
        def _(n):
            spread(n + 4, n, 64)

    @pl.when(blocks == 1)
    def _():
        @pl.loop(0, 2)
        def _(n):
            spread(n + 4, n, 64)
            spread(n + 2, n, 96)


def outer_fine_kernel(slab_blocks, points, arrived, inner, g, v, last, init, a, b):
    slab = lax.axis_index("tm")
    lane = lanes()
    taken = taker(points)

    def before(t, c, j, k):
        u = arrived[t, c, k]
        return pltpu.roll(u, 128 - 32 * j, 1) if j else u

    @pl.loop(0, 6)
    def _(t):
        @in_each
        def _(c, j, k):
            g[t + 2, c, j, k] = inner[t, c, j, k]

    def middle(t):
        @pl.when(t == 0)
        def _():
            start = (lane < 32) & (slab == 0)

            @in_each
            def _(c, j, k):
                a[c, j, k] = jnp.where(start, before(1, c, j, k), a[c, j, k])
                v[c, j, k] = 8.0 * a[c, j, k]

    def load(t, c, j, k):
        return jnp.where(lane < 32, before(t, c, j, k), pltpu.roll(taken(t, c, j, k), 32, 1))

    few = slab_blocks[slab] <= 2

    @pl.when(few)
    def _():
        @in_each
        def _(c, j, k):
            a[c, j, k] = load(1, c, j, k)

        @in_each
        def _(c, j, k):
            a[c, j, k] = jnp.where(lane < 64, load(0, c, j, k), pltpu.roll(a[c, j, k], 64, 1))

        chain(reader(a), a, b, g, 0, lambda: middle(0))

        @in_each
        def _(c, j, k):
            g[1, c, j, k] = pltpu.roll(g[0, c, j, k], 64, 1)

    @pl.when(jnp.logical_not(few))
    def _():
        @pl.loop(0, 2)
        def _(t):
            @in_each
            def _(c, j, k):
                a[c, j, k] = load(t, c, j, k)

            chain(reader(a), a, b, g, t, lambda: middle(t))

    eight_forced_steps(v, b, g)
    shift = 128 - 32 * (slab_blocks[slab] - 1)

    @rows_loop
    def _(k):
        for c in range(2):
            x = pltpu.roll(v[c, 0, k], shift % 128, 1)
            for j in range(1, 4):
                x = jnp.where(lane // 32 == j, pltpu.roll(v[c, j, k], (shift + 32 * j) % 128, 1), x)
            init[c, k] = 8.0 * arrived[1, c, k]
            last[c, k] = x


def second_pass_kernel(slab_blocks, v, arrived, init, g, big, left, right, a, b, coarse):
    slab = lax.axis_index("tm")
    lane = lanes()

    @rows_loop
    def _(k):
        for c in range(2):
            before = jnp.where(slab == 0, init[c, k], arrived[c, k])
            for j in range(4):
                head = before if j == 0 else pltpu.roll(before, 128 - 32 * j, 1)
                a[c, j, k] = jnp.where(lane < 32, head, pltpu.roll(v[c, j, k], 32, 1))

    quad_step(lambda c, j, k: 8.0 * a[c, j, k], writer(coarse), 2)
    eight_forced_steps(a, b, g)
    blocks = slab_blocks[slab]
    order = single_order()

    @rows_loop
    def _(k):
        for c in range(2):
            made = exchanged([8.0 * a[c, j, k] - coarse[c, j, k] for j in range(4)], (64, 32))
            for i in range(4):
                big[i, c, k] = made[i]

    @rows_loop
    def _(k):
        for c in range(2):
            for i in range(4):
                big[i, c, k] = jnp.where(i < blocks, picked(big[i, c, k], order), 0.0)

    @rows_loop
    def _(k):
        for c in range(2):
            made = [big[i, c, k] for i in range(4)]
            to_left, to_right = pltpu.roll(made[0], 96, 1), pltpu.roll(made[0], 64, 1)
            for i in range(4):
                if i:
                    to_left = jnp.where(lane // 32 == i, pltpu.roll(made[i], (32 * i + 96) % 128, 1), to_left)
                    to_right = jnp.where(lane // 32 == i, pltpu.roll(made[i], (32 * i + 64) % 128, 1), to_right)
            left[c, k] = to_left
            right[c, k] = to_right


def merge_kernel(
    slab_blocks, mine, mine_left, mine_right, mine_init, other, other_left, other_right, other_init, big, init, out
):
    lane = lanes()
    order = single_order()
    slab = lax.axis_index("tm")
    odd = slab % 2

    @rows_loop
    def _(k):
        for slot, centre, lower, upper in (
            (odd, mine, mine_left, mine_right),
            (1 - odd, other, other_left, other_right),
        ):
            for c in range(2):
                low, high = lower[c, k], upper[c, k]
                for i in range(4):
                    u = jnp.where(lane < 32, pltpu.roll(low, 128 - 32 * i, 1) if i else low, centre[i, c, k])
                    u = jnp.where(lane >= 96, pltpu.roll(high, 96 - 32 * i, 1) if i < 3 else high, u)
                    big[4 * slot + i, c, k] = u
        for c in range(2):
            init[c, k] = 8.0 * picked(jnp.where(odd == 1, other_init[c, k], mine_init[c, k]), order)

    sweep_kernel(0)(slab_blocks, init, big, out)


def sweep_kernel(plane):
    def kernel(slab_blocks, state, big, out):
        even = lax.axis_index("tm") // 2 * 2
        before = slab_blocks[even]

        @pl.when(even == 2 * plane)
        def _():
            def turn(n, s):
                slot = jnp.where(n < before, n, n - before + 4)
                p, q = step(s[0], s[1], 2)
                return p + big[slot, 0], q + big[slot, 1]

            p, q = lax.fori_loop(0, before + slab_blocks[even + 1], turn, (state[0], state[1]))
            out[0] = p
            out[1] = q

    kernel.__name__ = "sweep_kernel"
    return kernel


def solution_kernel(slab_blocks, state, big, heads, ends, solved):
    slab = lax.axis_index("tm")
    odd = slab % 2
    before = slab_blocks[slab - odd]
    order = quad_order()

    def turn(i, s):
        solved[jnp.maximum(i, 0), 0] = s[0]
        solved[jnp.maximum(i, 0), 1] = s[1]
        slot = jnp.where(i < 0, i + before, 4 * odd + i)
        p, q = step(s[0], s[1], 2)
        return p + big[slot, 0], q + big[slot, 1]

    p, q = lax.fori_loop(-odd * before, 4, turn, (state[0], state[1]))
    solved[4, 0] = p
    solved[4, 1] = q

    @rows_loop
    def _(k):
        for c in range(2):
            for i in range(5):
                solved[i, c, k] = picked(0.125 * solved[i, c, k], order)

    @rows_loop
    def _(k):
        for c in range(2):
            made = [solved[i, c, k] for i in range(5)]
            first, last = exchanged(made[:4], (64, 32)), exchanged(made[1:], (64, 32))
            for j in range(4):
                heads[c, j, k] = first[j]
                ends[c, j, k] = last[j]


def last_pass_kernel(slab_blocks, heads, ends, g, out, a, b):
    lane = lanes()
    flat = out.reshape(16 * 8 * 4 * 8, 128)
    scale = 1.0 / advection_rate[1]
    of_p = (lane % 32 >= 8) & (lane % 32 < 24)

    def put(t, ref):
        for j in range(4):
            for k in range(16):
                u = jnp.where(of_p, ref[0, j, k], pltpu.roll(ref[1, j, k], 16, 1))
                flat[pl.ds((k // 8) * 256 + t * 32 + j * 8 + k % 8, 8, stride=512), :] = scale * u

    @in_each
    def _(c, j, k):
        a[c, j, k] = heads[c, j, k]

    @pl.loop(0, 4)
    def _(n):
        quad_step(reader(a), adder(b, g, 2 * n), 1)
        put(2 * n, b)

        @pl.when(n < 3)
        def _():
            quad_step(reader(b), adder(a, g, 2 * n + 1), 1)
            put(2 * n + 1, a)

    put(7, ends)


def strips_kernel(slab_blocks, packed, out, made):
    lane = lanes()
    blocks = slab_blocks[lax.axis_index("tm")]
    order = (lane // 64 * 64 + 16 * (lane % 4) + lane % 64 // 4 + 8) % 128

    def stage(size):
        apart = size // 16
        lower = (lane + 120) % 128 // size % 2 == 0

        @pl.loop(0, 8, unroll=4)
        def _(t):
            for n in range(8):
                for x in range(8):
                    if x // apart % 2 == 0:
                        if size == 64:
                            p, q = packed[SNAKE[2 * n], t, x], packed[SNAKE[2 * n + 1], t, x]
                        else:
                            p, q = made[t, n, x], made[t, n, x + apart]
                        made[t, n, x] = jnp.where(lower, p, pltpu.roll(q, size, 1))
                        made[t, n, x + apart] = jnp.where(lower, pltpu.roll(p, 128 - size, 1), q)

    stage(64)
    stage(32)
    stage(16)

    @pl.loop(0, 8, unroll=4)
    def _(t):
        for n in range(8):
            for i in range(4):
                for c in range(2):
                    u = jnp.where(i < blocks, picked(made[t, n, 2 * i + c], order), 0.0)
                    out[8 * i + t, c, :, 128 * n : 128 * n + 128] = u


def body(init_field, guess, slab_blocks):
    ring = [(k, (k + 1) % 8) for k in range(8)]
    cores = [(k, k ^ 1) for k in range(8)]
    up = [(SNAKE[s], SNAKE[(s + 1) % 16]) for s in range(16)]
    down = [(SNAKE[(s + 1) % 16], SNAKE[s]) for s in range(16)]
    quad_scratch = pltpu.VMEM(QUAD, F32)

    slab = lax.axis_index("tm")
    kind = jnp.sum(jnp.where(jnp.arange(8) == slab, slab_blocks - 1, 0))

    def windows(nb):
        def branch(guess, init_field, slab_blocks):
            number = 2 * nb
            pieces = whole(
                windows_kernel(nb), shape(16, number, 2, 4, 8, 128), 2, 6, [pltpu.VMEM((2, 2 * number, 4, 8, 8, 128), F32)]
            )(slab_blocks, guess, init_field)
            points = lax.all_to_all(pieces, "space", 0, 0, tiled=True).reshape(16, number, 8, 8, 128)
            if nb == 4:
                return points
            return whole(gather_kernel(nb), shape(16, 8, 8, 8, 128), 1, 3)(slab_blocks, points)

        return branch

    def strips(nb):
        def branch(packed, slab_blocks):
            if nb < 4:
                packed = whole(pack_kernel(nb), shape(16, 2 * nb, 4, 8, 128), 1, 3)(slab_blocks, packed)
            packed = lax.all_to_all(packed, "space", 0, 0, tiled=True)
            if nb < 4:
                packed = whole(spread_kernel(nb), shape(16, 8, 4, 8, 128), 1, 3)(slab_blocks, packed)
            return packed

        return branch

    with jax.named_scope("column_windows"):
        points = lax.switch(kind, [windows(nb) for nb in (1, 2, 3, 4)], guess, init_field, slab_blocks)
        last_two = pl.BlockSpec((16, 2, 8, 8, 128), lambda i: (0, 3, 0, 0, 0))
        tail = whole(tail_kernel, shape(2, *SINGLE), (last_two,), 2, grid=(1,))(slab_blocks, points)
        before = lax.ppermute(tail, "tm", ring)

    with jax.named_scope("fine_and_first_pass"):
        fine = whole(inner_fine_kernel, shape(6, *QUAD), 1, 26, (quad_scratch, quad_scratch))(slab_blocks, points)
        g, v, last, init1 = whole(
            outer_fine_kernel,
            (shape(8, *QUAD), shape(*QUAD), shape(*SINGLE), shape(*SINGLE)),
            (last_two, None, None),
            12,
            (quad_scratch, quad_scratch),
            grid=(1,),
        )(slab_blocks, points, before, fine)
        arrived = lax.ppermute(last, "tm", ring[:-1])

    with jax.named_scope("second_pass"):
        big, left, right = whole(
            second_pass_kernel,
            (shape(4, *SINGLE), shape(*SINGLE), shape(*SINGLE)),
            4,
            4,
            (quad_scratch, quad_scratch, quad_scratch),
        )(slab_blocks, v, arrived, init1, g)

    with jax.named_scope("coarsest_level"):
        upper = lax.ppermute(left, "space", down)
        lower = lax.ppermute(right, "space", up)
        others = [lax.ppermute(x, "tm", cores) for x in (big, lower, upper, init1)]
        full, state, sent = whole(merge_kernel, (shape(8, *SINGLE), shape(*SINGLE), shape(*SINGLE)), 8, 2)(
            slab_blocks, big, lower, upper, init1, *others
        )
        plane = slab // 2
        for turn in range(3):
            if turn:
                sent = whole(sweep_kernel(turn), shape(*SINGLE), 2, 1)(slab_blocks, state, full)
            route = [(2 * turn + core, 2 * turn + 2 + core) for core in range(2)]
            came = lax.ppermute(sent, "tm", route)
            state = jnp.where(plane == turn + 1, came, state)

    with jax.named_scope("last_pass"):
        heads, ends = whole(
            solution_kernel, (shape(*QUAD), shape(*QUAD)), 2, 3, (pltpu.VMEM((5, *SINGLE), F32),)
        )(slab_blocks, state, full)
        packed = whole(last_pass_kernel, shape(16, 8, 4, 8, 128), 3, 6, (quad_scratch, quad_scratch))(
            slab_blocks, heads, ends, g
        )
        packed = lax.switch(kind, [strips(nb) for nb in (1, 2, 3, 4)], packed, slab_blocks)
        return whole(strips_kernel, shape(*guess.shape), 1, 5, (pltpu.VMEM((8, 8, 8, 8, 128), F32),))(
            slab_blocks, packed
        )


def solution(mesh):
    placed = (P(None, "space", None), P("tm", None, "space", None), P())
    return jax.shard_map(
        body, mesh=mesh, in_specs=placed, out_specs=P("tm", None, "space", None), check_vma=False
    )
```

profile of v0, /device:TPU:32, one launch (start us, length us, event | category | flops | bytes accessed | tf_op | source)
XLA Modules:
  0.0 164.3 jit_solution(8972728139590201729)
XLA Ops:
  0.0 1.3 fusion
  1.9 50.8 %conditional.2 = (f32[16,8,8,8,128]{4,3,2,1,0:T(8,128)}) conditional(s32[]{:T(128)} %clamp.4, (s32[8]{0:T(128)}, f32[32,2,8,1024]{3,2,1,0:T(8,128)}, f32[2,8,1024]{2,1,0:T(8,128)}) %tuple.29, (s32[8]{0:T(128)}, f32[32,2,8,1024]{3,2,1,0:T(8,128)}, f32[2,8,1024]{2,1,0:T(8,128)}) %tuple.29, (s32[8]{0:T(128)}, ...), branch_computations={%region_1.2_spmd, %region_2.3_spmd, %region_3.4_spmd, %region_4.5_... | conditional | flops 8999999488 | bytes 33291620 | solution.py:664
  2.0 6.0 %windows_kernel.7 = f32[16,8,2,4,8,128]{5,4,3,2,1,0:T(8,128)S(1)} custom-call(s32[8]{0:T(128)} %get-tuple-element.61.slab_blocks, f32[32,2,8,1024]{3,2,1,0:T(8,128)} %get-tuple-element.62.guess, f32[2,8,1024]{2,1,0:T(8,128)} %get-tuple-element.63.init), custom_call_target="tpu_custom_call" | custom-call | flops 6000000000 | bytes 18000000 | tf_op jit(solution)/shard_map/column_windows/cond/branch_3_fun/windows_kernel/pallas_call | solution.py:642
  8.0 44.7 %all_to_all.35 = f32[16,8,2,4,8,128]{5,4,3,2,1,0:T(8,128)} all-to-all(f32[16,8,2,4,8,128]{5,4,3,2,1,0:T(8,128)S(1)} %windows_kernel.7), channel_id=1, replica_groups=mesh['tm'=8,'space'=16] {'space'}, dimensions={0} | all-to-all | bytes 8388608 | tf_op jit(solution)/shard_map/column_windows/cond/branch_3_fun/all_to_all | solution.py:645
  52.7 0.0 copy-start.2
  52.7 0.0 copy-start.6
  52.7 2.2 %tail_kernel.1 = f32[2,2,16,8,128]{4,3,2,1,0:T(8,128)S(1)} custom-call(s32[8]{0:T(128)} %slab_blocks.19, f32[16,8,8,8,128]{4,3,2,1,0:T(8,128)} %get-tuple-element.94.points), custom_call_target="tpu_custom_call" | custom-call | flops 2000000000 | bytes 6000000 | tf_op jit(solution)/shard_map/column_windows/tail_kernel/pallas_call | solution.py:666
  54.9 0.0 collective-permute-start
  54.9 0.0 copy-done.2
  54.9 0.3 copy-done.6
  55.2 23.1 %inner_fine_kernel.1.inner = f32[6,2,4,16,8,128]{5,4,3,2,1,0:T(8,128)S(1)} custom-call(s32[8]{0:T(128)S(1)} %copy-done.2, f32[16,8,8,8,128]{4,3,2,1,0:T(8,128)S(1)} %copy-done.6), custom_call_target="tpu_custom_call" | custom-call | flops 25999998976 | bytes 78000000 | tf_op jit(solution)/shard_map/fine_and_first_pass/inner_fine_kernel/pallas_call | solution.py:670
  78.3 0.0 collective-permute-done.arrived
  78.3 11.3 %outer_fine_kernel.1 = (f32[8,2,4,16,8,128]{5,4,3,2,1,0:T(8,128)S(1)}, f32[2,4,16,8,128]{4,3,2,1,0:T(8,128)S(1)}, f32[2,16,8,128]{3,2,1,0:T(8,128)S(1)}, f32[2,16,8,128]{3,2,1,0:T(8,128)S(1)}) custom-call(s32[8]{0:T(128)S(1)} %copy-done.2, f32[16,8,8,8,128]{4,3,2,1,0:T(8,128)S(1)} %copy-done.6, f32[2,2,16,8,128]{4,3,2,1,0:T(8,128)S(1)} %collective-permute-done.arrived, ...), custom_call_target="tpu_custom_call" | custom-call | flops 12000000000 | bytes 36000000 | tf_op jit(solution)/shard_map/fine_and_first_pass/outer_fine_kernel/pallas_call | solution.py:671
  89.6 0.0 copy-start
  89.6 1.9 %collective-permute-start.1 = (f32[2,16,8,128]{3,2,1,0:T(8,128)S(1)}, f32[2,16,8,128]{3,2,1,0:T(8,128)S(1)}, u32[]{:S(2)}, u32[]{:S(2)}) collective-permute-start(f32[2,16,8,128]{3,2,1,0:T(8,128)S(1)} %get-tuple-element.83), channel_id=1, source_target_pairs={{0,16},{16,32},{32,48},{48,64},{64,80},{80,96},{96,112},{1,17},{17... | collective-permute-start | bytes 393224 | tf_op jit(solution)/shard_map/fine_and_first_pass/ppermute | solution.py:679
  91.5 4.4 %collective-permute-done.1.arrived = f32[2,16,8,128]{3,2,1,0:T(8,128)S(1)} collective-permute-done((f32[2,16,8,128]{3,2,1,0:T(8,128)S(1)}, f32[2,16,8,128]{3,2,1,0:T(8,128)S(1)}, u32[]{:S(2)}, u32[]{:S(2)}) %collective-permute-start.1) | collective-permute-done | bytes 131104 | tf_op jit(solution)/shard_map/fine_and_first_pass/ppermute | solution.py:679
  95.9 4.3 %second_pass_kernel.1 = (f32[4,2,16,8,128]{4,3,2,1,0:T(8,128)S(1)}, f32[2,16,8,128]{3,2,1,0:T(8,128)S(1)}, f32[2,16,8,128]{3,2,1,0:T(8,128)S(1)}) custom-call(s32[8]{0:T(128)S(1)} %copy-done.2, f32[2,4,16,8,128]{4,3,2,1,0:T(8,128)S(1)} %get-tuple-element.82.v, f32[2,16,8,128]{3,2,1,0:T(8,128)S(1)} %collective-permute-done.1.arrived, ...), custom_call_target="tpu_custom_call" | custom-call | flops 4000000000 | bytes 12000000 | tf_op jit(solution)/shard_map/second_pass/second_pass_kernel/pallas_call | solution.py:682
  100.2 0.0 copy-done
  100.2 0.1 collective-permute-start.4
  100.3 0.6 collective-permute-start.2
  100.9 2.7 %collective-permute-start.3 = (f32[2,16,8,128]{3,2,1,0:T(8,128)S(1)}, f32[2,16,8,128]{3,2,1,0:T(8,128)S(1)}, u32[]{:S(2)}, u32[]{:S(2)}) collective-permute-start(f32[2,16,8,128]{3,2,1,0:T(8,128)S(1)} %get-tuple-element.88), channel_id=1, source_target_pairs={{1,0},{2,1},{3,2},{7,3},{6,7},{5,6},{4,5},{8,4},{9,8},{10,9},{11,1... | collective-permute-start | bytes 393224 | tf_op jit(solution)/shard_map/coarsest_level/ppermute | solution.py:691
  103.6 0.0 collective-permute-start.7
  103.6 3.8 %collective-permute-done.2.mine_left = f32[2,16,8,128]{3,2,1,0:T(8,128)S(1)} collective-permute-done((f32[2,16,8,128]{3,2,1,0:T(8,128)S(1)}, f32[2,16,8,128]{3,2,1,0:T(8,128)S(1)}, u32[]{:S(2)}, u32[]{:S(2)}) %collective-permute-start.2) | collective-permute-done | bytes 131104 | tf_op jit(solution)/shard_map/coarsest_level/ppermute | solution.py:692
  107.4 0.0 collective-permute-start.5
  107.4 0.0 collective-permute-done.3.mine_right
  107.4 0.5 collective-permute-start.6
  107.9 0.0 collective-permute-done.7.other_init
  107.9 0.8 collective-permute-done.5.other_left
  108.7 0.2 collective-permute-done.6.other_right
  108.9 0.0 collective-permute-done.4.other
  108.9 1.1 merge_kernel.1
  110.1 1.3 collective-permute-start.8
  111.4 6.3 %collective-permute-done.8 = f32[2,16,8,128]{3,2,1,0:T(8,128)S(1)} collective-permute-done((f32[2,16,8,128]{3,2,1,0:T(8,128)S(1)}, f32[2,16,8,128]{3,2,1,0:T(8,128)S(1)}, u32[]{:S(2)}, u32[]{:S(2)}) %collective-permute-start.8) | collective-permute-done | bytes 131104 | tf_op jit(solution)/shard_map/coarsest_level/ppermute | solution.py:702
  117.7 1.5 sweep_kernel.2
  119.2 1.3 collective-permute-start.9
  120.6 2.7 %collective-permute-done.9 = f32[2,16,8,128]{3,2,1,0:T(8,128)S(1)} collective-permute-done((f32[2,16,8,128]{3,2,1,0:T(8,128)S(1)}, f32[2,16,8,128]{3,2,1,0:T(8,128)S(1)}, u32[]{:S(2)}, u32[]{:S(2)}) %collective-permute-start.9) | collective-permute-done | bytes 131104 | tf_op jit(solution)/shard_map/coarsest_level/ppermute | solution.py:702
  123.3 0.6 sweep_kernel.3
  123.8 0.7 collective-permute-start.10
  124.5 0.0 collective-permute-done.10
  124.6 0.0 copy-start.1
  124.6 3.8 %solution_kernel.1 = (f32[2,4,16,8,128]{4,3,2,1,0:T(8,128)S(1)}, f32[2,4,16,8,128]{4,3,2,1,0:T(8,128)S(1)}) custom-call(s32[8]{0:T(128)S(1)} %copy-done.2, f32[2,16,8,128]{3,2,1,0:T(8,128)S(1)} %broadcast_select_fusion.2.state, f32[8,2,16,8,128]{4,3,2,1,0:T(8,128)S(1)} %get-tuple-element.91.big), custom_call_target="tpu_custom_call" | custom-call | flops 3000000000 | bytes 9000000 | tf_op jit(solution)/shard_map/last_pass/solution_kernel/pallas_call | solution.py:706
  128.4 0.0 copy-done.1
  128.4 3.8 %last_pass_kernel.1 = f32[16,8,4,8,128]{4,3,2,1,0:T(8,128)S(1)} custom-call(s32[8]{0:T(128)S(1)} %copy-done.2, f32[2,4,16,8,128]{4,3,2,1,0:T(8,128)S(1)} %get-tuple-element.92.heads, f32[2,4,16,8,128]{4,3,2,1,0:T(8,128)S(1)} %get-tuple-element.93.ends, f32[8,2,4,16,8,128]{5,4,3,2,1,0:T(8,128)S(1)} %copy-done.1), custom_call_target="tpu_custom_call" | custom-call | flops 6000000000 | bytes 18000000 | tf_op jit(solution)/shard_map/last_pass/last_pass_kernel/pallas_call | solution.py:709
  132.2 27.5 %conditional.3 = (f32[16,8,4,8,128]{4,3,2,1,0:T(8,128)S(1)}) conditional(s32[]{:T(128)} %clamp.4, (s32[8]{0:T(128)S(1)}, f32[16,8,4,8,128]{4,3,2,1,0:T(8,128)S(1)}) %tuple.39, (s32[8]{0:T(128)S(1)}, f32[16,8,4,8,128]{4,3,2,1,0:T(8,128)S(1)}) %tuple.40, (s32[8]{0:T(128)S(1)}, ...), branch_computations={%region_5.6_spmd, %region_6.7_spmd, %region_7.8_spmd, %region_8.9_... | conditional | flops 6000000000 | bytes 21145736 | solution.py:712
  132.2 27.5 %all_to_all.39 = f32[16,8,4,8,128]{4,3,2,1,0:T(8,128)S(1)} all-to-all(f32[16,8,4,8,128]{4,3,2,1,0:T(8,128)S(1)} %param.7), channel_id=1, replica_groups=mesh['tm'=8,'space'=16] {'space'}, dimensions={0} | all-to-all | bytes 4194304 | tf_op jit(solution)/shard_map/last_pass/cond/branch_3_fun/all_to_all | solution.py:656
  159.7 4.6 %strips_kernel.1 = f32[32,2,8,1024]{3,2,1,0:T(8,128)} custom-call(s32[8]{0:T(128)S(1)} %copy-done.2, f32[16,8,4,8,128]{4,3,2,1,0:T(8,128)S(1)} %get-tuple-element.95.packed), custom_call_target="tpu_custom_call" | custom-call | flops 5000000000 | bytes 15000000 | tf_op jit(solution)/shard_map/last_pass/strips_kernel/pallas_call | solution.py:713
  (3 shorter events, 0.0 us)
Async XLA Ops:
  52.7 2.2 %copy-start.2 = (s32[8]{0:T(128)S(1)}, s32[8]{0:T(128)}, u32[]{:S(2)}) copy-start(s32[8]{0:T(128)} %slab_blocks.19) | copy-start | bytes 100
  52.7 2.5 %copy-start.6 = (f32[16,8,8,8,128]{4,3,2,1,0:T(8,128)S(1)}, f32[16,8,8,8,128]{4,3,2,1,0:T(8,128)}, u32[]{:S(2)}) copy-start(f32[16,8,8,8,128]{4,3,2,1,0:T(8,128)} %get-tuple-element.94.points) | copy-start | bytes 12582916
  54.9 23.4 %collective-permute-start = (f32[2,2,16,8,128]{4,3,2,1,0:T(8,128)S(1)}, f32[2,2,16,8,128]{4,3,2,1,0:T(8,128)S(1)}, u32[]{:S(2)}, u32[]{:S(2)}) collective-permute-start(f32[2,2,16,8,128]{4,3,2,1,0:T(8,128)S(1)} %tail_kernel.1), channel_id=1, source_target_pairs={{0,16},{16,32},{32,48},{48,64},{64,80},{80,96},{96,112},{112,0},{1... | collective-permute-start | bytes 786440 | tf_op jit(solution)/shard_map/column_windows/ppermute | solution.py:667
  89.6 10.6 %copy-start = (f32[8,2,4,16,8,128]{5,4,3,2,1,0:T(8,128)}, f32[8,2,4,16,8,128]{5,4,3,2,1,0:T(8,128)S(1)}, u32[]{:S(2)}) copy-start(f32[8,2,4,16,8,128]{5,4,3,2,1,0:T(8,128)S(1)} %get-tuple-element.85.g) | copy-start | bytes 12582916
  89.6 6.3 %collective-permute-start.1 = (f32[2,16,8,128]{3,2,1,0:T(8,128)S(1)}, f32[2,16,8,128]{3,2,1,0:T(8,128)S(1)}, u32[]{:S(2)}, u32[]{:S(2)}) collective-permute-start(f32[2,16,8,128]{3,2,1,0:T(8,128)S(1)} %get-tuple-element.83), channel_id=1, source_target_pairs={{0,16},{16,32},{32,48},{48,64},{64,80},{80,96},{96,112},{1,17},{17... | collective-permute-start | bytes 393224 | tf_op jit(solution)/shard_map/fine_and_first_pass/ppermute | solution.py:679
  100.2 8.8 %collective-permute-start.4 = (f32[4,2,16,8,128]{4,3,2,1,0:T(8,128)S(1)}, f32[4,2,16,8,128]{4,3,2,1,0:T(8,128)S(1)}, u32[]{:S(2)}, u32[]{:S(2)}) collective-permute-start(f32[4,2,16,8,128]{4,3,2,1,0:T(8,128)S(1)} %get-tuple-element.86.mine), channel_id=1, source_target_pairs={{0,16},{16,0},{32,48},{48,32},{64,80},{80,64},{96,112},{112,96},{1... | collective-permute-start | bytes 1572872 | tf_op jit(solution)/shard_map/coarsest_level/ppermute | solution.py:693
  100.3 7.1 %collective-permute-start.2 = (f32[2,16,8,128]{3,2,1,0:T(8,128)S(1)}, f32[2,16,8,128]{3,2,1,0:T(8,128)S(1)}, u32[]{:S(2)}, u32[]{:S(2)}) collective-permute-start(f32[2,16,8,128]{3,2,1,0:T(8,128)S(1)} %get-tuple-element.87), channel_id=1, source_target_pairs={{0,1},{1,2},{2,3},{3,7},{7,6},{6,5},{5,4},{4,8},{8,9},{9,10},{10,1... | collective-permute-start | bytes 393224 | tf_op jit(solution)/shard_map/coarsest_level/ppermute | solution.py:692
  100.9 6.5 %collective-permute-start.3 = (f32[2,16,8,128]{3,2,1,0:T(8,128)S(1)}, f32[2,16,8,128]{3,2,1,0:T(8,128)S(1)}, u32[]{:S(2)}, u32[]{:S(2)}) collective-permute-start(f32[2,16,8,128]{3,2,1,0:T(8,128)S(1)} %get-tuple-element.88), channel_id=1, source_target_pairs={{1,0},{2,1},{3,2},{7,3},{6,7},{5,6},{4,5},{8,4},{9,8},{10,9},{11,1... | collective-permute-start | bytes 393224 | tf_op jit(solution)/shard_map/coarsest_level/ppermute | solution.py:691
  103.6 4.3 %collective-permute-start.7 = (f32[2,16,8,128]{3,2,1,0:T(8,128)S(1)}, f32[2,16,8,128]{3,2,1,0:T(8,128)S(1)}, u32[]{:S(2)}, u32[]{:S(2)}) collective-permute-start(f32[2,16,8,128]{3,2,1,0:T(8,128)S(1)} %get-tuple-element.84.init.mine_init), channel_id=1, source_target_pairs={{0,16},{16,0},{32,48},{48,32},{64,80},{80,64},{96,112},{112,96},{1... | collective-permute-start | bytes 393224 | tf_op jit(solution)/shard_map/coarsest_level/ppermute | solution.py:693
  107.4 1.3 collective-permute-start.5
  107.4 1.5 collective-permute-start.6
  110.1 7.6 %collective-permute-start.8 = (f32[2,16,8,128]{3,2,1,0:T(8,128)S(1)}, f32[2,16,8,128]{3,2,1,0:T(8,128)S(1)}, u32[]{:S(2)}, u32[]{:S(2)}) collective-permute-start(f32[2,16,8,128]{3,2,1,0:T(8,128)S(1)} %get-tuple-element.89), channel_id=1, source_target_pairs={{0,32},{16,48},{1,33},{17,49},{2,34},{18,50},{3,35},{19,51},{4,36}... | collective-permute-start | bytes 393224 | tf_op jit(solution)/shard_map/coarsest_level/ppermute | solution.py:702
  119.2 4.0 %collective-permute-start.9 = (f32[2,16,8,128]{3,2,1,0:T(8,128)S(1)}, f32[2,16,8,128]{3,2,1,0:T(8,128)S(1)}, u32[]{:S(2)}, u32[]{:S(2)}) collective-permute-start(f32[2,16,8,128]{3,2,1,0:T(8,128)S(1)} %sweep_kernel.2), channel_id=1, source_target_pairs={{32,64},{48,80},{33,65},{49,81},{34,66},{50,82},{35,67},{51,83},{3... | collective-permute-start | bytes 393224 | tf_op jit(solution)/shard_map/coarsest_level/ppermute | solution.py:702
  123.8 0.7 collective-permute-start.10
  124.6 3.8 %copy-start.1 = (f32[8,2,4,16,8,128]{5,4,3,2,1,0:T(8,128)S(1)}, f32[8,2,4,16,8,128]{5,4,3,2,1,0:T(8,128)}, u32[]{:S(2)}) copy-start(f32[8,2,4,16,8,128]{5,4,3,2,1,0:T(8,128)} %copy-done) | copy-start | bytes 12582916
where the time goes:
time: 164 us
  blocking collectives  72.2 us (44%)
  Pallas kernels  62.2 us (38%)
  waiting for transfers between devices  18.2 us (11%)
  starting transfers between devices  9.1 us (6%)
    all_to_all x1, blocking collectives, branch(): lax.all_to_all(pieces, 'space', 0, 0, tiled=True)  44.7 us
    all_to_all x1, blocking collectives, branch(): packed = lax.all_to_all(packed, 'space', 0, 0, tiled=True)  27.5 us
    pallas_call x1, Pallas kernels, body(): whole(inner_fine_kernel, shape(6, *QUAD), 1, 26, (quad_scratch, quad_scra...  23.1 us
    pallas_call x1, Pallas kernels, body(): whole(outer_fine_kernel, (shape(8, *QUAD), shape(*QUAD), shape(*SINGLE),...  11.3 us
    ppermute x3, waiting for transfers between devices, body(): came = lax.ppermute(sent, 'tm', route)  9 us
    pallas_call x1, Pallas kernels, branch(): whole(windows_kernel(nb), shape(16, number, 2, 4, 8, 128), 2, 6, [pltpu.V...  6 us
    pallas_call x1, Pallas kernels, body(): whole(strips_kernel, shape(*guess.shape), 1, 5, (pltpu.VMEM((8, 8, 8, 8,...  4.59 us
    ppermute x1, waiting for transfers between devices, body(): arrived = lax.ppermute(last, 'tm', ring[:-1])  4.36 us
  transfers between devices with their start and end apart: 11, of which 6 were waited for; matrix products, arithmetic and copies ran while one was open for 0% of the time, Pallas kernels for 14%

commit v1 on v0

--- a/solution.py
+++ b/solution.py
@@ -218,7 +218,7 @@
     def kernel(slab_blocks, packed, out):
         group = lanes() // 32
 
-        @pl.loop(0, 16 * packed.shape[2], unroll=8)
+        @pl.loop(0, 16 * packed.shape[2], unroll=16)
         def _(m):
             source, x = m // packed.shape[2], m % packed.shape[2]
             us = [packed[source, n, x] for n in range(2 * nb)]
@@ -244,7 +244,7 @@
         group = (lanes() + 120) % 128 // 32
         if nb == 3:
 
-            @pl.loop(0, 16 * packed.shape[2], unroll=8)
+            @pl.loop(0, 16 * packed.shape[2], unroll=16)
             def _(m):
                 source, x = m // packed.shape[2], m % packed.shape[2]
                 us = [packed[source, n, x] for n in range(6)]
@@ -257,7 +257,7 @@
 
             return
 
-        @pl.loop(0, 16 * number, unroll=8)
+        @pl.loop(0, 16 * number, unroll=32)
         def _(m):
             source, n = m // number, m % number
             for x in range(packed.shape[2]):
@@ -276,7 +276,7 @@
         group = (lanes() + 120) % 128 // (32 if nb == 3 else 32 * nb)
         if nb == 3:
 
-            @pl.loop(0, 16 * full.shape[2], unroll=8)
+            @pl.loop(0, 16 * full.shape[2], unroll=16)
             def _(m):
                 target, x = m // full.shape[2], m % full.shape[2]
                 for n in range(6):
@@ -285,7 +285,7 @@
 
             return
 
-        @pl.loop(0, 16 * number, unroll=8)
+        @pl.loop(0, 16 * number, unroll=32)
         def _(m):
             target, n = m // number, m % number
             for x in range(full.shape[2]):

time: 164 us -> 159 us (0.970)
  the two profiles are of different devices: /device:TPU:32 before, /device:TPU:96 now
where the time goes in v1:
time: 159 us; the launch traced here: 158 us
  Pallas kernels  55.1 us (35%)
  waiting for transfers between devices  46 us (29%)
  blocking collectives  45.4 us (29%)
  starting transfers between devices  8.47 us (5%)
    all_to_all x1, blocking collectives, branch(): lax.all_to_all(pieces, 'space', 0, 0, tiled=True)  28.8 us
    ppermute x1, waiting for transfers between devices, body(): arrived = lax.ppermute(last, 'tm', ring[:-1])  25.2 us
    all_to_all x1, blocking collectives, branch(): packed = lax.all_to_all(packed, 'space', 0, 0, tiled=True)  16.6 us
    pallas_call x1, Pallas kernels, body(): whole(inner_fine_kernel, shape(6, *QUAD), 1, 26, (quad_scratch, quad_scra...  16.1 us
    ppermute x3, waiting for transfers between devices, body(): came = lax.ppermute(sent, 'tm', route)  13 us
    pallas_call x1, Pallas kernels, body(): whole(outer_fine_kernel, (shape(8, *QUAD), shape(*QUAD), shape(*SINGLE),...  8.09 us
    pallas_call x1, Pallas kernels, body(): whole(strips_kernel, shape(*guess.shape), 1, 5, (pltpu.VMEM((8, 8, 8, 8,...  4.59 us
    pallas_call x1, Pallas kernels, body(): whole(second_pass_kernel, (shape(4, *SINGLE), shape(*SINGLE), shape(*SING...  4.28 us
  transfers between devices with their start and end apart: 11, of which 6 were waited for; matrix products, arithmetic and copies ran while one was open for 0% of the time, Pallas kernels for 10%

profile of v1, /device:TPU:96, one launch (start us, length us, event | category | flops | bytes accessed | tf_op | source)
XLA Modules:
  0.0 157.6 jit_solution(17661105956886640003)
XLA Ops:
  0.0 1.3 fusion
  1.9 36.5 %conditional.2 = (f32[16,8,8,8,128]{4,3,2,1,0:T(8,128)}) conditional(s32[]{:T(128)} %clamp.4, (s32[8]{0:T(128)}, f32[32,2,8,1024]{3,2,1,0:T(8,128)}, f32[2,8,1024]{2,1,0:T(8,128)}) %tuple.29, (s32[8]{0:T(128)}, f32[32,2,8,1024]{3,2,1,0:T(8,128)}, f32[2,8,1024]{2,1,0:T(8,128)}) %tuple.29, (s32[8]{0:T(128)}, ...), branch_computations={%region_1.2_spmd, %region_2.3_spmd, %region_3.4_spmd, %region_4.5_... | conditional | flops 8999999488 | bytes 33291620 | solution.py:664
  2.0 3.8 %windows_kernel.5 = f32[16,4,2,4,8,128]{5,4,3,2,1,0:T(8,128)S(1)} custom-call(s32[8]{0:T(128)} %get-tuple-element.54.slab_blocks, f32[32,2,8,1024]{3,2,1,0:T(8,128)} %get-tuple-element.56.guess, f32[2,8,1024]{2,1,0:T(8,128)} %get-tuple-element.57.init), custom_call_target="tpu_custom_call" | custom-call | flops 6000000000 | bytes 18000000 | tf_op jit(solution)/shard_map/column_windows/cond/branch_1_fun/windows_kernel/pallas_call | solution.py:642
  5.8 0.0 copy-start.4
  5.8 28.8 %all_to_all.33 = f32[16,4,2,4,8,128]{5,4,3,2,1,0:T(8,128)S(1)} all-to-all(f32[16,4,2,4,8,128]{5,4,3,2,1,0:T(8,128)S(1)} %windows_kernel.5), channel_id=1, replica_groups=mesh['tm'=8,'space'=16] {'space'}, dimensions={0} | all-to-all | bytes 4194304 | tf_op jit(solution)/shard_map/column_windows/cond/branch_1_fun/all_to_all | solution.py:645
  34.6 0.0 copy-done.4
  34.6 3.9 %gather_kernel.4 = f32[16,8,8,8,128]{4,3,2,1,0:T(8,128)} custom-call(s32[8]{0:T(128)S(1)} %copy-done.4, f32[16,4,8,8,128]{4,3,2,1,0:T(8,128)S(1)} %bitcast.5), custom_call_target="tpu_custom_call" | custom-call | flops 3000000000 | bytes 9000000 | tf_op jit(solution)/shard_map/column_windows/cond/branch_1_fun/gather_kernel/pallas_call | solution.py:648
  38.5 2.2 %tail_kernel.1 = f32[2,2,16,8,128]{4,3,2,1,0:T(8,128)S(1)} custom-call(s32[8]{0:T(128)} %slab_blocks.19, f32[16,8,8,8,128]{4,3,2,1,0:T(8,128)} %get-tuple-element.94.points), custom_call_target="tpu_custom_call" | custom-call | flops 2000000000 | bytes 6000000 | tf_op jit(solution)/shard_map/column_windows/tail_kernel/pallas_call | solution.py:666
  40.7 0.0 collective-permute-start
  40.7 0.0 copy-done.2
  40.7 0.3 copy-done.6
  41.0 16.1 %inner_fine_kernel.1.inner = f32[6,2,4,16,8,128]{5,4,3,2,1,0:T(8,128)S(1)} custom-call(s32[8]{0:T(128)S(1)} %copy-done.2, f32[16,8,8,8,128]{4,3,2,1,0:T(8,128)S(1)} %copy-done.6), custom_call_target="tpu_custom_call" | custom-call | flops 25999998976 | bytes 78000000 | tf_op jit(solution)/shard_map/fine_and_first_pass/inner_fine_kernel/pallas_call | solution.py:670
  57.1 3.1 %collective-permute-done.arrived = f32[2,2,16,8,128]{4,3,2,1,0:T(8,128)S(1)} collective-permute-done((f32[2,2,16,8,128]{4,3,2,1,0:T(8,128)S(1)}, f32[2,2,16,8,128]{4,3,2,1,0:T(8,128)S(1)}, u32[]{:S(2)}, u32[]{:S(2)}) %collective-permute-start) | collective-permute-done | bytes 262176 | tf_op jit(solution)/shard_map/column_windows/ppermute | solution.py:667
  60.2 8.1 %outer_fine_kernel.1 = (f32[8,2,4,16,8,128]{5,4,3,2,1,0:T(8,128)S(1)}, f32[2,4,16,8,128]{4,3,2,1,0:T(8,128)S(1)}, f32[2,16,8,128]{3,2,1,0:T(8,128)S(1)}, f32[2,16,8,128]{3,2,1,0:T(8,128)S(1)}) custom-call(s32[8]{0:T(128)S(1)} %copy-done.2, f32[16,8,8,8,128]{4,3,2,1,0:T(8,128)S(1)} %copy-done.6, f32[2,2,16,8,128]{4,3,2,1,0:T(8,128)S(1)} %collective-permute-done.arrived, ...), custom_call_target="tpu_custom_call" | custom-call | flops 12000000000 | bytes 36000000 | tf_op jit(solution)/shard_map/fine_and_first_pass/outer_fine_kernel/pallas_call | solution.py:671
  68.2 0.0 copy-start
  68.3 1.9 %collective-permute-start.1 = (f32[2,16,8,128]{3,2,1,0:T(8,128)S(1)}, f32[2,16,8,128]{3,2,1,0:T(8,128)S(1)}, u32[]{:S(2)}, u32[]{:S(2)}) collective-permute-start(f32[2,16,8,128]{3,2,1,0:T(8,128)S(1)} %get-tuple-element.83), channel_id=1, source_target_pairs={{0,16},{16,32},{32,48},{48,64},{64,80},{80,96},{96,112},{1,17},{17... | collective-permute-start | bytes 393224 | tf_op jit(solution)/shard_map/fine_and_first_pass/ppermute | solution.py:679
  70.2 25.2 %collective-permute-done.1.arrived = f32[2,16,8,128]{3,2,1,0:T(8,128)S(1)} collective-permute-done((f32[2,16,8,128]{3,2,1,0:T(8,128)S(1)}, f32[2,16,8,128]{3,2,1,0:T(8,128)S(1)}, u32[]{:S(2)}, u32[]{:S(2)}) %collective-permute-start.1) | collective-permute-done | bytes 131104 | tf_op jit(solution)/shard_map/fine_and_first_pass/ppermute | solution.py:679
  95.3 4.3 %second_pass_kernel.1 = (f32[4,2,16,8,128]{4,3,2,1,0:T(8,128)S(1)}, f32[2,16,8,128]{3,2,1,0:T(8,128)S(1)}, f32[2,16,8,128]{3,2,1,0:T(8,128)S(1)}) custom-call(s32[8]{0:T(128)S(1)} %copy-done.2, f32[2,4,16,8,128]{4,3,2,1,0:T(8,128)S(1)} %get-tuple-element.82.v, f32[2,16,8,128]{3,2,1,0:T(8,128)S(1)} %collective-permute-done.1.arrived, ...), custom_call_target="tpu_custom_call" | custom-call | flops 4000000000 | bytes 12000000 | tf_op jit(solution)/shard_map/second_pass/second_pass_kernel/pallas_call | solution.py:682
  99.6 0.0 copy-done
  99.6 0.1 collective-permute-start.4
  99.7 0.6 collective-permute-start.2
  100.4 2.7 %collective-permute-start.3 = (f32[2,16,8,128]{3,2,1,0:T(8,128)S(1)}, f32[2,16,8,128]{3,2,1,0:T(8,128)S(1)}, u32[]{:S(2)}, u32[]{:S(2)}) collective-permute-start(f32[2,16,8,128]{3,2,1,0:T(8,128)S(1)} %get-tuple-element.88), channel_id=1, source_target_pairs={{1,0},{2,1},{3,2},{7,3},{6,7},{5,6},{4,5},{8,4},{9,8},{10,9},{11,1... | collective-permute-start | bytes 393224 | tf_op jit(solution)/shard_map/coarsest_level/ppermute | solution.py:691
  103.0 0.0 collective-permute-start.7
  103.0 3.8 %collective-permute-done.2.mine_left = f32[2,16,8,128]{3,2,1,0:T(8,128)S(1)} collective-permute-done((f32[2,16,8,128]{3,2,1,0:T(8,128)S(1)}, f32[2,16,8,128]{3,2,1,0:T(8,128)S(1)}, u32[]{:S(2)}, u32[]{:S(2)}) %collective-permute-start.2) | collective-permute-done | bytes 131104 | tf_op jit(solution)/shard_map/coarsest_level/ppermute | solution.py:692
  106.9 0.0 collective-permute-start.5
  106.9 0.0 collective-permute-done.3.mine_right
  106.9 0.5 collective-permute-start.6
  107.4 0.0 collective-permute-done.7.other_init
  107.4 0.8 collective-permute-done.5.other_left
  108.2 0.2 collective-permute-done.6.other_right
  108.4 0.0 collective-permute-done.4.other
  108.4 1.1 merge_kernel.1
  109.5 0.7 collective-permute-start.8
  110.2 0.0 collective-permute-done.8
  110.3 0.6 sweep_kernel.2
  110.8 0.7 collective-permute-start.9
  111.5 0.0 collective-permute-done.9
  111.6 0.6 sweep_kernel.3
  112.1 1.3 collective-permute-start.10
  113.4 13.0 %collective-permute-done.10 = f32[2,16,8,128]{3,2,1,0:T(8,128)S(1)} collective-permute-done((f32[2,16,8,128]{3,2,1,0:T(8,128)S(1)}, f32[2,16,8,128]{3,2,1,0:T(8,128)S(1)}, u32[]{:S(2)}, u32[]{:S(2)}) %collective-permute-start.10) | collective-permute-done | bytes 131104 | tf_op jit(solution)/shard_map/coarsest_level/ppermute | solution.py:702
  126.4 0.0 copy-start.1
  126.4 3.8 %solution_kernel.1 = (f32[2,4,16,8,128]{4,3,2,1,0:T(8,128)S(1)}, f32[2,4,16,8,128]{4,3,2,1,0:T(8,128)S(1)}) custom-call(s32[8]{0:T(128)S(1)} %copy-done.2, f32[2,16,8,128]{3,2,1,0:T(8,128)S(1)} %broadcast_select_fusion.2.state, f32[8,2,16,8,128]{4,3,2,1,0:T(8,128)S(1)} %get-tuple-element.91.big), custom_call_target="tpu_custom_call" | custom-call | flops 3000000000 | bytes 9000000 | tf_op jit(solution)/shard_map/last_pass/solution_kernel/pallas_call | solution.py:706
  130.3 3.8 %last_pass_kernel.1 = f32[16,8,4,8,128]{4,3,2,1,0:T(8,128)S(1)} custom-call(s32[8]{0:T(128)S(1)} %copy-done.2, f32[2,4,16,8,128]{4,3,2,1,0:T(8,128)S(1)} %get-tuple-element.92.heads, f32[2,4,16,8,128]{4,3,2,1,0:T(8,128)S(1)} %get-tuple-element.93.ends, f32[8,2,4,16,8,128]{5,4,3,2,1,0:T(8,128)S(1)} %copy-done.1), custom_call_target="tpu_custom_call" | custom-call | flops 6000000000 | bytes 18000000 | tf_op jit(solution)/shard_map/last_pass/last_pass_kernel/pallas_call | solution.py:709
  134.1 18.9 %conditional.3 = (f32[16,8,4,8,128]{4,3,2,1,0:T(8,128)S(1)}) conditional(s32[]{:T(128)} %clamp.4, (s32[8]{0:T(128)S(1)}, f32[16,8,4,8,128]{4,3,2,1,0:T(8,128)S(1)}) %tuple.39, (s32[8]{0:T(128)S(1)}, f32[16,8,4,8,128]{4,3,2,1,0:T(8,128)S(1)}) %tuple.40, (s32[8]{0:T(128)S(1)}, ...), branch_computations={%region_5.6_spmd, %region_6.7_spmd, %region_7.8_spmd, %region_8.9_... | conditional | flops 6000000000 | bytes 21145736 | solution.py:712
  134.1 1.2 pack_kernel.4
  135.3 16.6 %all_to_all.37.packed = f32[16,4,4,8,128]{4,3,2,1,0:T(8,128)S(1)} all-to-all(f32[16,4,4,8,128]{4,3,2,1,0:T(8,128)S(1)} %pack_kernel.4), channel_id=1, replica_groups=mesh['tm'=8,'space'=16] {'space'}, dimensions={0} | all-to-all | bytes 2097152 | tf_op jit(solution)/shard_map/last_pass/cond/branch_1_fun/all_to_all | solution.py:656
  151.8 1.2 spread_kernel.4
  153.0 4.6 %strips_kernel.1 = f32[32,2,8,1024]{3,2,1,0:T(8,128)} custom-call(s32[8]{0:T(128)S(1)} %copy-done.2, f32[16,8,4,8,128]{4,3,2,1,0:T(8,128)S(1)} %get-tuple-element.95.packed), custom_call_target="tpu_custom_call" | custom-call | flops 5000000000 | bytes 15000000 | tf_op jit(solution)/shard_map/last_pass/strips_kernel/pallas_call | solution.py:713
  (6 shorter events, 0.1 us)
Async XLA Ops:
  5.8 28.8 %copy-start.4 = (s32[8]{0:T(128)S(1)}, s32[8]{0:T(128)}, u32[]{:S(2)}) copy-start(s32[8]{0:T(128)} %get-tuple-element.54.slab_blocks) | copy-start | bytes 100 | tf_op jit(solution)/shard_map/column_windows/cond
  38.5 2.2 %copy-start.2 = (s32[8]{0:T(128)S(1)}, s32[8]{0:T(128)}, u32[]{:S(2)}) copy-start(s32[8]{0:T(128)} %slab_blocks.19) | copy-start | bytes 100
  38.5 2.5 %copy-start.6 = (f32[16,8,8,8,128]{4,3,2,1,0:T(8,128)S(1)}, f32[16,8,8,8,128]{4,3,2,1,0:T(8,128)}, u32[]{:S(2)}) copy-start(f32[16,8,8,8,128]{4,3,2,1,0:T(8,128)} %get-tuple-element.94.points) | copy-start | bytes 12582916
  40.7 19.5 %collective-permute-start = (f32[2,2,16,8,128]{4,3,2,1,0:T(8,128)S(1)}, f32[2,2,16,8,128]{4,3,2,1,0:T(8,128)S(1)}, u32[]{:S(2)}, u32[]{:S(2)}) collective-permute-start(f32[2,2,16,8,128]{4,3,2,1,0:T(8,128)S(1)} %tail_kernel.1), channel_id=1, source_target_pairs={{0,16},{16,32},{32,48},{48,64},{64,80},{80,96},{96,112},{112,0},{1... | collective-permute-start | bytes 786440 | tf_op jit(solution)/shard_map/column_windows/ppermute | solution.py:667
  68.2 31.4 %copy-start = (f32[8,2,4,16,8,128]{5,4,3,2,1,0:T(8,128)}, f32[8,2,4,16,8,128]{5,4,3,2,1,0:T(8,128)S(1)}, u32[]{:S(2)}) copy-start(f32[8,2,4,16,8,128]{5,4,3,2,1,0:T(8,128)S(1)} %get-tuple-element.85.g) | copy-start | bytes 12582916
  68.3 27.1 %collective-permute-start.1 = (f32[2,16,8,128]{3,2,1,0:T(8,128)S(1)}, f32[2,16,8,128]{3,2,1,0:T(8,128)S(1)}, u32[]{:S(2)}, u32[]{:S(2)}) collective-permute-start(f32[2,16,8,128]{3,2,1,0:T(8,128)S(1)} %get-tuple-element.83), channel_id=1, source_target_pairs={{0,16},{16,32},{32,48},{48,64},{64,80},{80,96},{96,112},{1,17},{17... | collective-permute-start | bytes 393224 | tf_op jit(solution)/shard_map/fine_and_first_pass/ppermute | solution.py:679
  99.6 8.8 %collective-permute-start.4 = (f32[4,2,16,8,128]{4,3,2,1,0:T(8,128)S(1)}, f32[4,2,16,8,128]{4,3,2,1,0:T(8,128)S(1)}, u32[]{:S(2)}, u32[]{:S(2)}) collective-permute-start(f32[4,2,16,8,128]{4,3,2,1,0:T(8,128)S(1)} %get-tuple-element.86.mine), channel_id=1, source_target_pairs={{0,16},{16,0},{32,48},{48,32},{64,80},{80,64},{96,112},{112,96},{1... | collective-permute-start | bytes 1572872 | tf_op jit(solution)/shard_map/coarsest_level/ppermute | solution.py:693
  99.7 7.1 %collective-permute-start.2 = (f32[2,16,8,128]{3,2,1,0:T(8,128)S(1)}, f32[2,16,8,128]{3,2,1,0:T(8,128)S(1)}, u32[]{:S(2)}, u32[]{:S(2)}) collective-permute-start(f32[2,16,8,128]{3,2,1,0:T(8,128)S(1)} %get-tuple-element.87), channel_id=1, source_target_pairs={{0,1},{1,2},{2,3},{3,7},{7,6},{6,5},{5,4},{4,8},{8,9},{9,10},{10,1... | collective-permute-start | bytes 393224 | tf_op jit(solution)/shard_map/coarsest_level/ppermute | solution.py:692
  100.4 6.5 %collective-permute-start.3 = (f32[2,16,8,128]{3,2,1,0:T(8,128)S(1)}, f32[2,16,8,128]{3,2,1,0:T(8,128)S(1)}, u32[]{:S(2)}, u32[]{:S(2)}) collective-permute-start(f32[2,16,8,128]{3,2,1,0:T(8,128)S(1)} %get-tuple-element.88), channel_id=1, source_target_pairs={{1,0},{2,1},{3,2},{7,3},{6,7},{5,6},{4,5},{8,4},{9,8},{10,9},{11,1... | collective-permute-start | bytes 393224 | tf_op jit(solution)/shard_map/coarsest_level/ppermute | solution.py:691
  103.0 4.3 %collective-permute-start.7 = (f32[2,16,8,128]{3,2,1,0:T(8,128)S(1)}, f32[2,16,8,128]{3,2,1,0:T(8,128)S(1)}, u32[]{:S(2)}, u32[]{:S(2)}) collective-permute-start(f32[2,16,8,128]{3,2,1,0:T(8,128)S(1)} %get-tuple-element.84.init.mine_init), channel_id=1, source_target_pairs={{0,16},{16,0},{32,48},{48,32},{64,80},{80,64},{96,112},{112,96},{1... | collective-permute-start | bytes 393224 | tf_op jit(solution)/shard_map/coarsest_level/ppermute | solution.py:693
  106.9 1.3 collective-permute-start.5
  106.9 1.5 collective-permute-start.6
  109.5 0.7 collective-permute-start.8
  110.8 0.7 collective-permute-start.9
  112.1 14.3 %collective-permute-start.10 = (f32[2,16,8,128]{3,2,1,0:T(8,128)S(1)}, f32[2,16,8,128]{3,2,1,0:T(8,128)S(1)}, u32[]{:S(2)}, u32[]{:S(2)}) collective-permute-start(f32[2,16,8,128]{3,2,1,0:T(8,128)S(1)} %sweep_kernel.3), channel_id=1, source_target_pairs={{64,96},{80,112},{65,97},{81,113},{66,98},{82,114},{67,99},{83,115... | collective-permute-start | bytes 393224 | tf_op jit(solution)/shard_map/coarsest_level/ppermute | solution.py:702
  126.4 3.8 %copy-start.1 = (f32[8,2,4,16,8,128]{5,4,3,2,1,0:T(8,128)S(1)}, f32[8,2,4,16,8,128]{5,4,3,2,1,0:T(8,128)}, u32[]{:S(2)}) copy-start(f32[8,2,4,16,8,128]{5,4,3,2,1,0:T(8,128)} %copy-done) | copy-start | bytes 12582916
